TPU v7x, 32 devices: a whole 2x2x4 slice. The times are simulated.
32 devices in a mesh: cells: 4 (over z), grow: 4 (over x, core), gcol: 2 (over y).
Axes of the slice: x: 2, y: 2, z: 4, core: 2. Of those that a mesh axis runs over, the one named last changes fastest.
Arguments:
- counts: int32 [4608, 4, 2, 1024], P('cells', 'grow', 'gcol'), may hold values from 0 to 2689, as said below
- gene_mean: float32 [4, 2, 1024], P('grow', 'gcol'), may hold values from 0.2 to 1.2
- gene_scale: float32 [4, 2, 1024], P('grow', 'gcol'), may hold values from 0.4 to 2
Outputs:
- coexpression: float32 [4, 2048, 2, 4, 1024], P('grow', 'cells', 'gcol')
Inputs may be any that keep to these rules, and one draw needn't show every extreme that they name: `counts`: every cell has at least one count.
All inputs are finite; a program needn't handle non-finite values.
Results may differ from a plain program's by a relative error of at most 0.0008.
Values may be sent and summed in bfloat16 or wider, within the bound.
A program may use at most 384 MiB of HBM per device.

v0:
```python
import jax
import jax.numpy as jnp
from jax import lax
from jax.sharding import PartitionSpec as P

GENES = 8192


def per_device(counts, gene_mean, gene_scale):
    cell_rows = counts.shape[0]
    width = counts.shape[3]
    local = counts.reshape(cell_rows, width).astype(jnp.float32)
    partial_totals = jnp.sum(local, axis=1)
    totals = lax.psum(partial_totals, ("grow", "gcol"))
    lognorm = jnp.log1p(local * GENES / totals[:, None])
    standard = ((lognorm - gene_mean.reshape(1, width)) / gene_scale.reshape(1, width)).astype(
        jnp.bfloat16
    )
    n_grow = lax.axis_size("grow")
    n_gcol = lax.axis_size("gcol")
    row_values = lax.all_gather(standard.reshape(cell_rows, 1, width), "gcol", axis=1, tiled=True)
    col_values = lax.all_gather(standard.reshape(cell_rows, 1, width), "grow", axis=1, tiled=True)
    row_flat = row_values.reshape(cell_rows, n_gcol * width)
    col_flat = col_values.reshape(cell_rows, n_grow * width)
    panel_rows = row_flat.shape[1]
    n_cells = lax.axis_size("cells")
    owned = panel_rows // n_cells
    summed = lax.psum_scatter(
        lax.dot_general(
            row_flat, col_flat, (((0,), (0,)), ((), ())), preferred_element_type=jnp.float32
        ),
        "cells",
        scatter_dimension=0,
        tiled=True,
    )
    scaled = summed / (n_cells * cell_rows)
    return scaled.reshape(1, owned, 1, n_grow, width)


def solution(mesh):
    placed = (P("cells", "grow", "gcol", None), P("grow", "gcol", None), P("grow", "gcol", None))
    return jax.shard_map(
        per_device,
        mesh=mesh,
        in_specs=placed,
        out_specs=P("grow", "cells", "gcol", None, None),
        check_vma=False,
    )
```

profile of v0, /device:TPU:4, one launch (start us, length us, event | category | flops | bytes accessed | tf_op | source)
XLA Modules:
  0.0 777.4 jit_solution(4910621642717855920)
XLA Ops:
  6.5 0.0 copy-start
  6.5 0.0 copy-start.1
  6.5 0.0 all-gather.3.cloned.1.call-start
  6.5 3.1 fusion.4
  9.6 12.4 %psum.7 = f32[1152]{0:T(1024)S(1)} all-reduce(f32[1152]{0:T(1024)S(1)} %fusion.4), channel_id=1, replica_groups=mesh['cells'=4,'grow'=4,'gcol'=2] {'grow','gcol'}, use_global_device_ids=true, to_apply=%region_1.0 | all-reduce | flops 1152 | bytes 9216 | tf_op jit(solution)/shard_map/psum | solution.py:14
  22.1 0.0 copy-done
  22.1 0.0 copy-done.1
  22.1 5.6 fusion.3
  27.7 0.0 all-gather.3.cloned.1.call-update
  27.7 0.0 all-gather.5.cloned.1.call-start
  27.8 0.7 all-gather.5.cloned.1.call-update
  28.5 0.0 reduce-scatter.2.cloned.1.call-start
  28.5 62.6 %all-gather.3.cloned.1.call-done = bf16[1152,2,1024]{2,0,1:T(8,128)(2,1)} async-done(((bf16[1152,1,1024]{2,0,1:T(8,128)(2,1)}), bf16[1152,2,1024]{2,0,1:T(8,128)(2,1)}) %all-gather.3.cloned.1.call-update) | async-done | bytes 4718608 | tf_op jit(solution)/shard_map/all_gather | solution.py:21
  91.1 6.6 copy.8
  97.8 60.4 %all-gather.5.cloned.1.call-done = bf16[1152,4,1024]{2,0,1:T(8,128)(2,1)} async-done(((bf16[1152,1,1024]{2,0,1:T(8,128)(2,1)}), bf16[1152,4,1024]{2,0,1:T(8,128)(2,1)}) %all-gather.5.cloned.1.call-update) | async-done | bytes 9437200 | tf_op jit(solution)/shard_map/all_gather | solution.py:22
  158.1 12.6 %copy.9 = bf16[1152,4,1024]{0,2,1:T(8,128)(2,1)} copy(bf16[1152,4,1024]{2,0,1:T(8,128)(2,1)} %all-gather.5.cloned.1.call-done) | data formatting | bytes 18874368 | tf_op jit(solution)/shard_map/all_gather | solution.py:22
  170.8 29.0 %fusion.5 = f32[2048,4096]{1,0:T(8,128)} fusion(bf16[1152,2048]{0,1:T(8,128)(2,1)} %bitcast.18, bf16[1152,4096]{0,1:T(8,128)(2,1)} %bitcast.17), kind=kOutput, calls=%fused_computation.8 | convolution fusion | flops 19327352832 | bytes 47710208 | tf_op jit(solution)/shard_map/dot_general | solution.py:29
  199.7 0.0 reduce-scatter.2.cloned.1.call-update
  199.8 552.2 %reduce-scatter.2.cloned.1.call-done = f32[512,4096]{1,0:T(8,128)} async-done(((f32[2048,4096]{1,0:T(8,128)}), f32[512,4096]{1,0:T(8,128)}) %reduce-scatter.2.cloned.1.call-update) | async-done | bytes 8388624 | tf_op jit(solution)/shard_map/reduce_scatter | solution.py:28
  752.0 8.1 %broadcast_multiply_fusion = f32[512,4096]{1,0:T(8,128)} fusion(f32[512,4096]{1,0:T(8,128)} %reduce-scatter.2.cloned.1.call-done), kind=kLoop, calls=%fused_computation.7 | loop fusion | flops 2097152 | bytes 16777216 | tf_op jit(solution)/shard_map/div | solution.py:36
  760.1 10.8 %reshape.124 = f32[1,512,1,4,1024]{4,3,1,2,0:T(4,128)} reshape(f32[512,4096]{1,0:T(8,128)} %broadcast_multiply_fusion) | data formatting | bytes 16777216 | tf_op jit(solution)/shard_map/reshape | solution.py:37
Async XLA Ops:
  6.5 15.5 %copy-start = (f32[1,1,1024]{2,1,0:T(1,128)S(1)}, f32[1,1,1024]{2,1,0:T(1,128)}, u32[]{:S(2)}) copy-start(f32[1,1,1024]{2,1,0:T(1,128)} %param.5) | copy-start | bytes 12292
  6.5 15.5 %copy-start.1 = (f32[1,1,1024]{2,1,0:T(1,128)S(1)}, f32[1,1,1024]{2,1,0:T(1,128)}, u32[]{:S(2)}) copy-start(f32[1,1,1024]{2,1,0:T(1,128)} %param.4) | copy-start | bytes 12292
  6.5 84.6 %all-gather.3.cloned.1.call-start = ((), (), s32[]{:S(2)}) async-start(), calls=%async_computation.1 | async-start | bytes 7077888 | tf_op jit(solution)/shard_map/all_gather | solution.py:21
  27.7 130.4 %all-gather.5.cloned.1.call-start = ((), (), s32[]{:S(2)}) async-start(), calls=%async_computation.2 | async-start | bytes 11796480 | tf_op jit(solution)/shard_map/all_gather | solution.py:22
  28.5 723.5 %reduce-scatter.2.cloned.1.call-start = ((), (), s32[]{:S(2)}) async-start(), calls=%async_computation.3 | async-start | bytes 41943040 | tf_op jit(solution)/shard_map/reduce_scatter | solution.py:28
Sparse Core Ops, SparseCore 0:
  27.8 63.2 all-gather.2
  92.7 65.3 all-gather.4
  199.9 552.0 reduce-scatter.1
where the time goes:
time: 780 us; the launch traced here: 777 us
  waiting for transfers between devices  676 us (87%)
  local copies, waits for them, and re-layouts  30.1 us (4%)
  matrix products  29 us (4%)
  other arithmetic  16.8 us (2%)
  between operations  13.1 us (2%)
  blocking collectives  12.4 us (2%)
    reduce_scatter x1, waiting for transfers between devices, per_device(): lax.psum_scatter(lax.dot_general(row_flat, col_flat, (((0,), (0,)), ((),...  552 us
    all_gather x1, waiting for transfers between devices, per_device(): lax.all_gather(standard.reshape(cell_rows, 1, width), 'gcol', axis=1, til...  62.6 us
    all_gather x1, waiting for transfers between devices, per_device(): lax.all_gather(standard.reshape(cell_rows, 1, width), 'grow', axis=1, til...  60.4 us
    dot_general x1, matrix products, per_device(): lax.dot_general(row_flat, col_flat, (((0,), (0,)), ((), ())), preferred_e...  29 us
  transfers between devices with their start and end apart: 3, of which 3 were waited for; matrix products, arithmetic and copies ran while one was open for 1% of the time, Pallas kernels for 0%

commit v1 on v0

v1 whole, which is shorter than its diff:
```python
import functools

import jax
import jax.numpy as jnp
from jax import lax
from jax.experimental import pallas as pl
from jax.experimental.pallas import tpu as pltpu
from jax.sharding import PartitionSpec as P

GENES = 8192
MESH = pl.DeviceIdType.MESH
SIB, UP, DOWN, ACROSS = range(4)
TILE = 256


def standardize(counts, gene_mean, gene_scale):
    cell_rows, width = counts.shape[0], counts.shape[3]
    local = counts.reshape(cell_rows, width).astype(jnp.float32)
    totals = lax.psum(jnp.sum(local, axis=1), ("grow", "gcol"))
    lognorm = jnp.log1p(local * GENES / totals[:, None])
    return ((lognorm - gene_mean.reshape(1, width)) / gene_scale.reshape(1, width)).astype(
        jnp.bfloat16
    )


def gram_kernel(nz, rows, cuts, std_ref, out_ref, xs, landed, turned, acc,
                load_sem, recv_sem, send_sem, rows_recv, rows_send, out_sem):
    zi, gi, yi = lax.axis_index("cells"), lax.axis_index("grow"), lax.axis_index("gcol")
    width = xs.shape[3]
    last = nz - 1
    x, c = gi // 2, gi % 2
    g_sib = x * 2 + (1 - c)
    g_across = (1 - x) * 2 + c
    target = {
        SIB: {"grow": g_sib},
        UP: {"cells": jnp.minimum(zi + 1, last)},
        DOWN: {"cells": jnp.maximum(zi - 1, 0)},
        ACROSS: {"grow": g_across},
    }
    owner = (zi * 2) // nz == yi
    own_col = pl.multiple_of((zi % (nz // 2)) * rows, rows)

    barrier = pltpu.get_barrier_semaphore()

    def greet(to):
        pl.semaphore_signal(barrier, inc=1, device_id=to, device_id_type=MESH)

    greet(target[SIB])
    greet(target[ACROSS])
    greet({"gcol": 1 - yi})
    pl.when(zi < last)(lambda: greet(target[UP]))
    pl.when(zi > 0)(lambda: greet(target[DOWN]))
    load = pltpu.make_async_copy(std_ref, xs.at[zi, gi], load_sem)
    load.start()
    ends_of_line = (zi == 0).astype(jnp.int32) + (zi == last).astype(jnp.int32)
    pl.semaphore_wait(barrier, 5 - ends_of_line)

    def part(h):
        return pl.ds(cuts[h], cuts[h + 1] - cuts[h])

    def copy(kind, z, g, h):
        ref = xs.at[z, g, part(h), :]
        return pltpu.make_async_remote_copy(
            src_ref=ref, dst_ref=ref,
            send_sem=send_sem.at[kind, z, g // 2, h], recv_sem=recv_sem.at[z, g, h],
            device_id=target[kind], device_id_type=MESH,
        )

    def rows_copy(z, h):
        return pltpu.make_async_remote_copy(
            src_ref=xs.at[z, gi, part(h), pl.ds(own_col, rows)], dst_ref=landed.at[z, part(h), :],
            send_sem=rows_send.at[z, h], recv_sem=rows_recv.at[z, h],
            device_id={"gcol": 1 - yi}, device_id_type=MESH,
        )

    def sends(z, mine, h, act):
        g = gi if mine else g_across
        if mine:
            pl.when((z <= zi) & (zi < last))(lambda: act(copy(UP, z, g, h)))
            pl.when((z >= zi) & (zi > 0))(lambda: act(copy(DOWN, z, g, h)))
            if h == 0:
                act(copy(ACROSS, z, g, h))
            else:
                by_line = ((z == 0) & (zi != 0)) | ((z == last) & (zi != last))
                pl.when(jnp.logical_not(by_line))(lambda: act(copy(ACROSS, z, g, h)))
            pl.when(owner)(lambda: act(rows_copy(z, h)))
        elif h == 1:
            pl.when((z == 0) & (zi < last))(lambda: act(copy(UP, z, g, h)))
            pl.when((z == last) & (zi > 0))(lambda: act(copy(DOWN, z, g, h)))
        act(copy(SIB, z, g, h))

    def start(dma):
        dma.start()

    def finish(dma):
        dma.wait_send()

    def arrive(z, g, h):
        copy(SIB, z, g, h).wait_recv()

    def place(d, side):
        z = zi - d + 2 * d * side
        valid = (z >= 0) & (z <= last) & ((d > 0) | (side == 0))
        return z, valid

    def forward(d):
        for h in range(2):
            for side in range(2):
                z, valid = place(d, side)

                @pl.when(valid)
                def _():
                    pl.when(d > 0)(lambda: arrive(z, gi, h))
                    sends(z, True, h, start)

    def ends(d):
        for z, hit in ((0, zi == d - 1), (last, last - zi == d - 1)):
            @pl.when(hit)
            def _():
                arrive(z, g_across, 1)
                sends(z, False, 1, start)

    def turn(z, h):
        for k in range(cuts[h], cuts[h + 1], 128):
            @pl.when(owner)
            def _():
                turned[z, :, k:k + 128] = xs[z, gi, k:k + 128, pl.ds(own_col, rows)].T

            @pl.when(jnp.logical_not(owner))
            def _():
                turned[z, :, k:k + 128] = landed[z, k:k + 128, :].T

    def multiply(z, g, h):
        tiles = width // TILE

        def body(i, carry):
            a = (g // 2) * 2 + i // tiles
            n = pl.ds(pl.multiple_of((i % tiles) * TILE, TILE), TILE)
            acc[a, :, n] += jnp.dot(
                turned[z, :, part(h)], xs[z, a, part(h), n], preferred_element_type=jnp.float32
            )
            return carry

        lax.fori_loop(0, 2 * tiles, body, 0)

    def near(d):
        def body(side, carry):
            z, valid = place(d, side)

            @pl.when(valid)
            def _():
                for h in range(2):
                    pl.when(jnp.logical_not(owner))(lambda: rows_copy(z, h).wait_recv())
                    turn(z, h)
                    arrive(z, g_sib, h)
                    multiply(z, gi, h)
            return carry

        lax.fori_loop(0, 2, body, 0)

    def far(d):
        def body(side, carry):
            z, valid = place(d, side)

            @pl.when(valid)
            def _():
                for h in range(2):
                    def take():
                        arrive(z, g_across, h)
                        start(copy(SIB, z, g_across, h))
                    if h == 0:
                        take()
                    else:
                        pl.when((z > 0) & (z < last))(take)
                    arrive(z, (1 - x) * 2 + (1 - c), h)
                    multiply(z, g_across, h)
            return carry

        lax.fori_loop(0, 2, body, 0)

    acc[...] = jnp.zeros_like(acc)
    load.wait()

    def step(d, carry):
        pl.when(d < nz)(lambda: forward(d))
        ends(d)
        pl.when(d < nz)(lambda: near(d))
        pl.when(d > 0)(lambda: far(d - 1))
        return carry

    lax.fori_loop(0, nz + 1, step, 0)

    outs = [
        pltpu.make_async_copy(acc.at[a], out_ref.at[:, a, :], out_sem.at[a])
        for a in range(acc.shape[0])
    ]
    for dma in outs:
        dma.start()

    def drain(z, carry):
        for h in range(2):
            for mine in (True, False):
                sends(z, mine, h, finish)
        return carry

    lax.fori_loop(0, nz, drain, 0)
    for dma in outs:
        dma.wait()


def line_plan(counts, gene_mean, gene_scale):
    nz, n_grow = lax.axis_size("cells"), lax.axis_size("grow")
    cell_rows, width = counts.shape[0], counts.shape[3]
    standard = standardize(counts, gene_mean, gene_scale)
    rows = 2 * width // nz
    cuts = (0, -(-cell_rows // 256) * 128, cell_rows)
    flops = 2 * rows * n_grow * width * nz * cell_rows
    summed = pl.pallas_call(
        functools.partial(gram_kernel, nz, rows, cuts),
        out_shape=jax.ShapeDtypeStruct((rows, n_grow, width), jnp.float32),
        in_specs=[pl.BlockSpec(memory_space=pl.ANY)],
        out_specs=pl.BlockSpec(memory_space=pl.ANY),
        scratch_shapes=[
            pltpu.VMEM((nz, n_grow, cell_rows, width), jnp.bfloat16),
            pltpu.VMEM((nz, cell_rows, rows), jnp.bfloat16),
            pltpu.VMEM((nz, rows, cell_rows), jnp.bfloat16),
            pltpu.VMEM((n_grow, rows, width), jnp.float32),
            pltpu.SemaphoreType.DMA,
            pltpu.SemaphoreType.DMA((nz, n_grow, 2)),
            pltpu.SemaphoreType.DMA((4, nz, 2, 2)),
            pltpu.SemaphoreType.DMA((nz, 2)),
            pltpu.SemaphoreType.DMA((nz, 2)),
            pltpu.SemaphoreType.DMA((n_grow,)),
        ],
        compiler_params=pltpu.CompilerParams(
            collective_id=0, has_side_effects=True, vmem_limit_bytes=60 * 2**20
        ),
        cost_estimate=pl.CostEstimate(
            flops=flops, bytes_accessed=4 * rows * n_grow * width, transcendentals=0
        ),
    )(standard)
    return (summed / (nz * cell_rows)).reshape(1, rows, 1, n_grow, width)


def sum_plan(counts, gene_mean, gene_scale):
    cell_rows, width = counts.shape[0], counts.shape[3]
    standard = standardize(counts, gene_mean, gene_scale).reshape(cell_rows, 1, width)
    n_grow, n_gcol, n_cells = (lax.axis_size(a) for a in ("grow", "gcol", "cells"))
    row_flat = lax.all_gather(standard, "gcol", axis=1, tiled=True).reshape(cell_rows, -1)
    col_flat = lax.all_gather(standard, "grow", axis=1, tiled=True).reshape(cell_rows, -1)
    owned = row_flat.shape[1] // n_cells
    summed = lax.psum_scatter(
        lax.dot_general(
            row_flat, col_flat, (((0,), (0,)), ((), ())), preferred_element_type=jnp.float32
        ),
        "cells",
        scatter_dimension=0,
        tiled=True,
    )
    return (summed / (n_cells * cell_rows)).reshape(1, owned, 1, n_grow, width)


def solution(mesh):
    placed = (P("cells", "grow", "gcol", None), P("grow", "gcol", None), P("grow", "gcol", None))
    sizes = tuple(mesh.shape[a] for a in ("cells", "grow", "gcol"))
    return jax.shard_map(
        line_plan if sizes == (4, 4, 2) else sum_plan,
        mesh=mesh,
        in_specs=placed,
        out_specs=P("grow", "cells", "gcol", None, None),
        check_vma=False,
    )
```

time: 780 us -> 230 us (0.29)
  waiting for transfers between devices: 676 us -> 0 us
  Pallas kernels: 0 us -> 196 us
  local copies, waits for them, and re-layouts: 30.1 us -> 0.01 us
  matrix products: 29 us -> 0 us
  between operations: 13.1 us -> 0.03 us
    reduce_scatter x1 -> x0, waiting for transfers between devices: 552 us -> none  [per_device(): lax.psum_scatter(lax.dot_general(row_flat, col_flat, (((0,), (0,)), ((),...]
    pallas_call x0 -> x1, Pallas kernels: none -> 196 us  [line_plan(): pl.pallas_call(functools.partial(gram_kernel, nz, rows, cuts), out_shape=...]
    all_gather x2 -> x0, waiting for transfers between devices: 123 us -> none  [the longest x1 62.6 us: per_device(): lax.all_gather(standard.reshape(cell_rows, 1, width), 'gcol', axis=1, til...]
    dot_general x1 -> x0, matrix products: 29 us -> none  [per_device(): lax.dot_general(row_flat, col_flat, (((0,), (0,)), ((), ())), preferred_e...]
    all_gather x2 -> x0, local copies, waits for them, and re-layouts: 19.2 us -> none  [the longest x1 12.6 us: per_device(): lax.all_gather(standard.reshape(cell_rows, 1, width), 'grow', axis=1, til...]
    reshape x1 -> x0, local copies, waits for them, and re-layouts: 10.8 us -> none  [per_device(): return scaled.reshape(1, owned, 1, n_grow, width)]
    reshape x0 -> x1, other arithmetic: none -> 9.56 us  [line_plan(): return (summed / (nz * cell_rows)).reshape(1, rows, 1, n_grow, width)]
    div x1 -> x0, other arithmetic: 8.1 us -> none  [per_device(): scaled = summed / (n_cells * cell_rows)]
  transfers between devices with their start and end apart: 3 -> 0, of which waited for: 3 -> 0; matrix products, arithmetic and copies ran while one was open for 1% -> 0% of each run, Pallas kernels for 0% -> 0%
where the time goes in v1:
time: 230 us; the launch traced here: 226 us
  Pallas kernels  196 us (85%)
  other arithmetic  18.2 us (8%)
  blocking collectives  12.4 us (5%)
    pallas_call x1, Pallas kernels, line_plan(): pl.pallas_call(functools.partial(gram_kernel, nz, rows, cuts), out_shape=...  196 us
    psum x1, blocking collectives, standardize(): totals = lax.psum(jnp.sum(local, axis=1), ('grow', 'gcol'))  12.4 us
    reshape x1, other arithmetic, line_plan(): return (summed / (nz * cell_rows)).reshape(1, rows, 1, n_grow, width)  9.56 us
    convert_element_type x1, other arithmetic, standardize(): ((lognorm - gene_mean.reshape(1, width)) / gene_scale.reshape(1, width))....  5.58 us

profile of v1, /device:TPU:4, one launch (start us, length us, event | category | flops | bytes accessed | tf_op | source)
XLA Modules:
  0.0 226.3 jit_solution(2210975939578971391)
XLA Ops:
  0.0 0.0 copy-start
  0.0 0.0 copy-start.1
  0.0 3.1 %fusion.4 = f32[1152]{0:T(1024)S(1)} fusion(s32[1152,1,1,1024]{3,2,1,0:T(1,128)} %param.3), kind=kLoop, calls=%fused_computation.7 | loop fusion | flops 2358144 | bytes 4723200 | tf_op jit(solution)/shard_map/reduce_sum | solution.py:19
  3.1 12.4 %psum.7 = f32[1152]{0:T(1024)S(1)} all-reduce(f32[1152]{0:T(1024)S(1)} %fusion.4), channel_id=1, replica_groups=mesh['cells'=4,'grow'=4,'gcol'=2] {'grow','gcol'}, use_global_device_ids=true, to_apply=%region_1.0 | all-reduce | flops 1152 | bytes 9216 | tf_op jit(solution)/shard_map/psum | solution.py:19
  15.5 0.0 copy-done
  15.5 0.0 copy-done.1
  15.5 5.6 %fusion.3.std_ref = bf16[1152,1024]{1,0:T(8,128)(2,1)} fusion(s32[1152,1,1,1024]{3,2,1,0:T(1,128)} %param.3, f32[1024]{0:T(1024)S(1)} %bitcast.16, f32[1024]{0:T(1024)S(1)} %bitcast.17, f32[1152]{0:T(1024)S(1)} %psum.7), kind=kLoop, calls=%fused_computation.6 | loop fusion | flops 7077888 | bytes 7090688 | tf_op jit(solution)/shard_map/convert_element_type | solution.py:21
  21.1 195.6 %shard_map.37 = f32[512,4,1024]{2,1,0:T(4,128)} custom-call(bf16[1152,1024]{1,0:T(8,128)(2,1)} %fusion.3.std_ref), custom_call_target="tpu_custom_call" | custom-call | flops 19327352832 | bytes 8388608 | tf_op jit(solution)/shard_map/pallas_call | solution.py:218
  216.8 9.6 %multiply_bitcast_fusion = f32[1,512,1,4,1024]{4,3,2,1,0:T(4,128)} fusion(f32[512,4,1024]{2,1,0:T(4,128)} %shard_map.37), kind=kLoop, calls=%fused_computation | loop fusion | flops 2097152 | bytes 16777216 | tf_op jit(solution)/shard_map/reshape | solution.py:242
Async XLA Ops:
  0.0 15.5 %copy-start = (f32[1,1,1024]{2,1,0:T(1,128)S(1)}, f32[1,1,1024]{2,1,0:T(1,128)}, u32[]{:S(2)}) copy-start(f32[1,1,1024]{2,1,0:T(1,128)} %param.5) | copy-start | bytes 12292
  0.0 15.5 %copy-start.1 = (f32[1,1,1024]{2,1,0:T(1,128)S(1)}, f32[1,1,1024]{2,1,0:T(1,128)}, u32[]{:S(2)}) copy-start(f32[1,1,1024]{2,1,0:T(1,128)} %param.4) | copy-start | bytes 12292

commit v2 on v1

--- a/solution.py
+++ b/solution.py
@@ -23,8 +23,9 @@
     )
 
 
-def gram_kernel(nz, rows, cuts, std_ref, out_ref, xs, landed, turned, acc,
-                load_sem, recv_sem, send_sem, rows_recv, rows_send, out_sem):
+def gram_kernel(nz, rows, cuts, counts_ref, mean_ref, scale_ref, out_ref,
+                staged, sums, heard, xs, landed, turned, acc,
+                load_sem, sums_recv, sums_send, recv_sem, send_sem, rows_recv, rows_send, out_sem):
     zi, gi, yi = lax.axis_index("cells"), lax.axis_index("grow"), lax.axis_index("gcol")
     width = xs.shape[3]
     last = nz - 1
@@ -45,15 +46,23 @@
     def greet(to):
         pl.semaphore_signal(barrier, inc=1, device_id=to, device_id_type=MESH)
 
-    greet(target[SIB])
-    greet(target[ACROSS])
-    greet({"gcol": 1 - yi})
+    peers = [
+        {"grow": (gi + dg) % 4, "gcol": (yi + dy) % 2}
+        for dg in range(4) for dy in range(2) if dg or dy
+    ]
+    for peer in peers:
+        greet(peer)
     pl.when(zi < last)(lambda: greet(target[UP]))
     pl.when(zi > 0)(lambda: greet(target[DOWN]))
-    load = pltpu.make_async_copy(std_ref, xs.at[zi, gi], load_sem)
-    load.start()
-    ends_of_line = (zi == 0).astype(jnp.int32) + (zi == last).astype(jnp.int32)
-    pl.semaphore_wait(barrier, 5 - ends_of_line)
+    loads = [
+        pltpu.make_async_copy(
+            counts_ref.at[pl.ds(cuts[h], cuts[h + 1] - cuts[h]), 0, :],
+            staged.at[pl.ds(cuts[h], cuts[h + 1] - cuts[h]), :], load_sem.at[h],
+        )
+        for h in range(2)
+    ]
+    for dma in loads:
+        dma.start()
 
     def part(h):
         return pl.ds(cuts[h], cuts[h + 1] - cuts[h])
@@ -162,40 +171,93 @@
         def body(side, carry):
             z, valid = place(d, side)
 
+            def take(h):
+                arrive(z, g_across, h)
+                start(copy(SIB, z, g_across, h))
+
+            def use(h):
+                arrive(z, (1 - x) * 2 + (1 - c), h)
+                multiply(z, g_across, h)
+
+            at_end = (z == 0) | (z == last)
+
             @pl.when(valid)
             def _():
-                for h in range(2):
-                    def take():
-                        arrive(z, g_across, h)
-                        start(copy(SIB, z, g_across, h))
-                    if h == 0:
-                        take()
-                    else:
-                        pl.when((z > 0) & (z < last))(take)
-                    arrive(z, (1 - x) * 2 + (1 - c), h)
-                    multiply(z, g_across, h)
+                pl.when(at_end)(lambda: use(1))
+                take(0)
+                use(0)
+
+                @pl.when(jnp.logical_not(at_end))
+                def _():
+                    take(1)
+                    use(1)
             return carry
 
         lax.fori_loop(0, 2, body, 0)
 
+    def add_up(k, carry):
+        r = pl.ds(pl.multiple_of(k * 128, 128), 128)
+        total = staged[r, 0:128].astype(jnp.float32)
+        for j in range(128, width, 128):
+            total += staged[r, j:j + 128].astype(jnp.float32)
+        sums[pl.ds(k, 1), :] = jnp.sum(total.T, axis=0, keepdims=True)
+        return carry
+
+    def standardize_rows(k, carry):
+        r = pl.ds(pl.multiple_of(k * 128, 128), 128)
+        share = GENES / jnp.broadcast_to(sums[pl.ds(k, 1), :], (128, 128)).T
+        for j in range(0, width, 128):
+            lognorm = jnp.log1p(staged[r, j:j + 128].astype(jnp.float32) * share)
+            xs[zi, gi, r, j:j + 128] = (
+                (lognorm - mean_ref[:, j:j + 128]) / scale_ref[:, j:j + 128]
+            ).astype(jnp.bfloat16)
+        return carry
+
+    sums[...] = jnp.zeros_like(sums)
+    for h in range(2):
+        loads[h].wait()
+        lax.fori_loop(cuts[h] // 128, cuts[h + 1] // 128, add_up, 0)
+    ends_of_line = (zi == 0).astype(jnp.int32) + (zi == last).astype(jnp.int32)
+    pl.semaphore_wait(barrier, len(peers) + 2 - ends_of_line)
+    tells = [
+        pltpu.make_async_remote_copy(
+            src_ref=sums, dst_ref=heard.at[i], send_sem=sums_send.at[i], recv_sem=sums_recv.at[i],
+            device_id=peer, device_id_type=MESH,
+        )
+        for i, peer in enumerate(peers)
+    ]
+    for dma in tells:
+        dma.start()
+    for dma in tells:
+        dma.wait()
+    whole = sums[...]
+    for i in range(len(peers)):
+        whole += heard[i]
+    sums[...] = whole
+    for h in range(2):
+        lax.fori_loop(cuts[h] // 128, cuts[h + 1] // 128, standardize_rows, 0)
+        sends(zi, True, h, start)
     acc[...] = jnp.zeros_like(acc)
-    load.wait()
+
+    def deliver(a):
+        acc[a] = acc[a] * (1.0 / (nz * cuts[2]))
+        pltpu.make_async_copy(acc.at[a], out_ref.at[:, a, :], out_sem.at[a]).start()
 
     def step(d, carry):
-        pl.when(d < nz)(lambda: forward(d))
+        @pl.when(d == nz)
+        def _():
+            deliver(gi)
+            deliver(g_sib)
+
+        pl.when((d > 0) & (d < nz))(lambda: forward(d))
         ends(d)
         pl.when(d < nz)(lambda: near(d))
         pl.when(d > 0)(lambda: far(d - 1))
         return carry
 
     lax.fori_loop(0, nz + 1, step, 0)
-
-    outs = [
-        pltpu.make_async_copy(acc.at[a], out_ref.at[:, a, :], out_sem.at[a])
-        for a in range(acc.shape[0])
-    ]
-    for dma in outs:
-        dma.start()
+    deliver(g_across)
+    deliver((1 - x) * 2 + (1 - c))
 
     def drain(z, carry):
         for h in range(2):
@@ -204,28 +266,51 @@
         return carry
 
     lax.fori_loop(0, nz, drain, 0)
-    for dma in outs:
+    for a in range(acc.shape[0]):
+        pltpu.make_async_copy(acc.at[a], out_ref.at[:, a, :], out_sem.at[a]).wait()
+
+
+def copy_kernel(src, dst, sems):
+    n = sems.shape[0]
+    each = src.shape[0] // n
+    dmas = [
+        pltpu.make_async_copy(
+            src.at[pl.ds(i * each, each)], dst.at[pl.ds(i * each, each)], sems.at[i]
+        )
+        for i in range(n)
+    ]
+    for dma in dmas:
+        dma.start()
+    for dma in dmas:
         dma.wait()
 
 
 def line_plan(counts, gene_mean, gene_scale):
     nz, n_grow = lax.axis_size("cells"), lax.axis_size("grow")
     cell_rows, width = counts.shape[0], counts.shape[3]
-    standard = standardize(counts, gene_mean, gene_scale)
     rows = 2 * width // nz
     cuts = (0, -(-cell_rows // 256) * 128, cell_rows)
     flops = 2 * rows * n_grow * width * nz * cell_rows
-    summed = pl.pallas_call(
+    scaled = pl.pallas_call(
         functools.partial(gram_kernel, nz, rows, cuts),
         out_shape=jax.ShapeDtypeStruct((rows, n_grow, width), jnp.float32),
-        in_specs=[pl.BlockSpec(memory_space=pl.ANY)],
+        in_specs=[
+            pl.BlockSpec(memory_space=pl.ANY),
+            pl.BlockSpec(memory_space=pltpu.VMEM),
+            pl.BlockSpec(memory_space=pltpu.VMEM),
+        ],
         out_specs=pl.BlockSpec(memory_space=pl.ANY),
         scratch_shapes=[
+            pltpu.VMEM((cell_rows, width), jnp.int32),
+            pltpu.VMEM((-(-cell_rows // 1024) * 8, 128), jnp.float32),
+            pltpu.VMEM((7, -(-cell_rows // 1024) * 8, 128), jnp.float32),
             pltpu.VMEM((nz, n_grow, cell_rows, width), jnp.bfloat16),
             pltpu.VMEM((nz, cell_rows, rows), jnp.bfloat16),
             pltpu.VMEM((nz, rows, cell_rows), jnp.bfloat16),
             pltpu.VMEM((n_grow, rows, width), jnp.float32),
-            pltpu.SemaphoreType.DMA,
+            pltpu.SemaphoreType.DMA((2,)),
+            pltpu.SemaphoreType.DMA((7,)),
+            pltpu.SemaphoreType.DMA((7,)),
             pltpu.SemaphoreType.DMA((nz, n_grow, 2)),
             pltpu.SemaphoreType.DMA((4, nz, 2, 2)),
             pltpu.SemaphoreType.DMA((nz, 2)),
@@ -233,13 +318,20 @@
             pltpu.SemaphoreType.DMA((n_grow,)),
         ],
         compiler_params=pltpu.CompilerParams(
-            collective_id=0, has_side_effects=True, vmem_limit_bytes=60 * 2**20
+            collective_id=0, has_side_effects=True, vmem_limit_bytes=62 * 2**20
         ),
         cost_estimate=pl.CostEstimate(
             flops=flops, bytes_accessed=4 * rows * n_grow * width, transcendentals=0
         ),
-    )(standard)
-    return (summed / (nz * cell_rows)).reshape(1, rows, 1, n_grow, width)
+    )(counts.reshape(cell_rows, 1, width), gene_mean.reshape(1, width), gene_scale.reshape(1, width))
+    copied = pl.pallas_call(
+        copy_kernel,
+        out_shape=jax.ShapeDtypeStruct(scaled.shape, scaled.dtype),
+        in_specs=[pl.BlockSpec(memory_space=pl.ANY)],
+        out_specs=pl.BlockSpec(memory_space=pl.ANY),
+        scratch_shapes=[pltpu.SemaphoreType.DMA((8,))],
+    )(scaled)
+    return copied.reshape(1, rows, 1, n_grow, width)
 
 
 def sum_plan(counts, gene_mean, gene_scale):

time: 230 us -> 460 us (2.00)
  Pallas kernels: 196 us -> 459 us
  other arithmetic: 18.2 us -> 0 us
  blocking collectives: 12.4 us -> 0 us
    pallas_call x0 -> x1, Pallas kernels: none -> 255 us  [line_plan(): pl.pallas_call(copy_kernel, out_shape=jax.ShapeDtypeStruct(scaled.shape,...]
    psum x1 -> x0, blocking collectives: 12.4 us -> none  [standardize(): totals = lax.psum(jnp.sum(local, axis=1), ('grow', 'gcol'))]
    reshape x1 -> x0, other arithmetic: 9.56 us -> none  [line_plan(): return (summed / (nz * cell_rows)).reshape(1, rows, 1, n_grow, width)]
    pallas_call x1, Pallas kernels: 196 us -> 204 us  [line_plan(): pl.pallas_call(functools.partial(gram_kernel, nz, rows, cuts), out_shape=...]
    convert_element_type x1 -> x0, other arithmetic: 5.58 us -> none  [standardize(): ((lognorm - gene_mean.reshape(1, width)) / gene_scale.reshape(1, width))....]
where the time goes in v2:
time: 460 us; the launch traced here: 459 us
  Pallas kernels  459 us (100%)
    pallas_call x1, Pallas kernels, line_plan(): pl.pallas_call(copy_kernel, out_shape=jax.ShapeDtypeStruct(scaled.shape,...  255 us
    pallas_call x1, Pallas kernels, line_plan(): pl.pallas_call(functools.partial(gram_kernel, nz, rows, cuts), out_shape=...  204 us

profile of v2, /device:TPU:4, one launch (start us, length us, event | category | flops | bytes accessed | tf_op | source)
XLA Modules:
  0.0 459.5 jit_solution(10845829214505089794)
XLA Ops:
  0.0 204.2 %shard_map.37.src = f32[512,4,1024]{2,1,0:T(4,128)} custom-call(s32[1152,1,1024]{2,1,0:T(1,128)} %bitcast.6, f32[1,1024]{1,0:T(1,128)} %bitcast.7, f32[1,1024]{1,0:T(1,128)} %bitcast.8), custom_call_target="tpu_custom_call" | custom-call | flops 19327352832 | bytes 8388608 | tf_op jit(solution)/shard_map/pallas_call | solution.py:294
  204.2 255.3 %shard_map.38 = f32[512,4,1024]{2,1,0:T(4,128)} custom-call(f32[512,4,1024]{2,1,0:T(4,128)} %shard_map.37.src), custom_call_target="tpu_custom_call" | custom-call | tf_op jit(solution)/shard_map/pallas_call | solution.py:327

commit v3 on v2

--- a/solution.py
+++ b/solution.py
@@ -270,18 +270,18 @@
         pltpu.make_async_copy(acc.at[a], out_ref.at[:, a, :], out_sem.at[a]).wait()
 
 
-def copy_kernel(src, dst, sems):
-    n = sems.shape[0]
+def copy_kernel(src, dst, held, load_sems, store_sems):
+    n = load_sems.shape[0]
     each = src.shape[0] // n
-    dmas = [
-        pltpu.make_async_copy(
-            src.at[pl.ds(i * each, each)], dst.at[pl.ds(i * each, each)], sems.at[i]
-        )
-        for i in range(n)
-    ]
-    for dma in dmas:
+    at = [pl.ds(i * each, each) for i in range(n)]
+    loads = [pltpu.make_async_copy(src.at[r], held.at[r], load_sems.at[i]) for i, r in enumerate(at)]
+    stores = [pltpu.make_async_copy(held.at[r], dst.at[r], store_sems.at[i]) for i, r in enumerate(at)]
+    for dma in loads:
         dma.start()
-    for dma in dmas:
+    for load, store in zip(loads, stores):
+        load.wait()
+        store.start()
+    for dma in stores:
         dma.wait()
 
 
@@ -289,7 +289,7 @@
     nz, n_grow = lax.axis_size("cells"), lax.axis_size("grow")
     cell_rows, width = counts.shape[0], counts.shape[3]
     rows = 2 * width // nz
-    cuts = (0, -(-cell_rows // 256) * 128, cell_rows)
+    cuts = (0, cell_rows // 256 * 128, cell_rows)
     flops = 2 * rows * n_grow * width * nz * cell_rows
     scaled = pl.pallas_call(
         functools.partial(gram_kernel, nz, rows, cuts),
@@ -329,7 +329,12 @@
         out_shape=jax.ShapeDtypeStruct(scaled.shape, scaled.dtype),
         in_specs=[pl.BlockSpec(memory_space=pl.ANY)],
         out_specs=pl.BlockSpec(memory_space=pl.ANY),
-        scratch_shapes=[pltpu.SemaphoreType.DMA((8,))],
+        scratch_shapes=[
+            pltpu.VMEM(scaled.shape, scaled.dtype),
+            pltpu.SemaphoreType.DMA((16,)),
+            pltpu.SemaphoreType.DMA((16,)),
+        ],
+        compiler_params=pltpu.CompilerParams(vmem_limit_bytes=62 * 2**20),
     )(scaled)
     return copied.reshape(1, rows, 1, n_grow, width)
 

time: 460 us -> 214 us (0.47)
  Pallas kernels: 459 us -> 214 us
    pallas_call x1, Pallas kernels: 255 us -> 6.57 us  [line_plan(): pl.pallas_call(copy_kernel, out_shape=jax.ShapeDtypeStruct(scaled.shape,...]
where the time goes in v3:
time: 214 us
  Pallas kernels  214 us (100%)
    pallas_call x1, Pallas kernels, line_plan(): pl.pallas_call(functools.partial(gram_kernel, nz, rows, cuts), out_shape=...  207 us
    pallas_call x1, Pallas kernels, line_plan(): pl.pallas_call(copy_kernel, out_shape=jax.ShapeDtypeStruct(scaled.shape,...  6.57 us

profile of v3, /device:TPU:4, one launch (start us, length us, event | category | flops | bytes accessed | tf_op | source)
XLA Modules:
  0.0 214.0 jit_solution(6534920362503837246)
XLA Ops:
  0.0 207.4 %shard_map.37.src = f32[512,4,1024]{2,1,0:T(4,128)} custom-call(s32[1152,1,1024]{2,1,0:T(1,128)} %bitcast.6, f32[1,1024]{1,0:T(1,128)} %bitcast.7, f32[1,1024]{1,0:T(1,128)} %bitcast.8), custom_call_target="tpu_custom_call" | custom-call | flops 19327352832 | bytes 8388608 | tf_op jit(solution)/shard_map/pallas_call | solution.py:294
  207.4 6.6 %shard_map.38 = f32[512,4,1024]{2,1,0:T(4,128)} custom-call(f32[512,4,1024]{2,1,0:T(4,128)} %shard_map.37.src), custom_call_target="tpu_custom_call" | custom-call | tf_op jit(solution)/shard_map/pallas_call | solution.py:327

commit v4 on v3

--- a/solution.py
+++ b/solution.py
@@ -23,15 +23,17 @@
     )
 
 
-def gram_kernel(nz, rows, cuts, counts_ref, mean_ref, scale_ref, out_ref,
+def gram_kernel(nz, rows, cuts, m, counts_ref, mean_ref, scale_ref, out_ref,
                 staged, sums, heard, xs, landed, turned, acc,
                 load_sem, sums_recv, sums_send, recv_sem, send_sem, rows_recv, rows_send, out_sem):
     zi, gi, yi = lax.axis_index("cells"), lax.axis_index("grow"), lax.axis_index("gcol")
     width = xs.shape[3]
     last = nz - 1
+    parts = len(cuts) - 1
     x, c = gi // 2, gi % 2
     g_sib = x * 2 + (1 - c)
     g_across = (1 - x) * 2 + c
+    g_other = (1 - x) * 2 + (1 - c)
     target = {
         SIB: {"grow": g_sib},
         UP: {"cells": jnp.minimum(zi + 1, last)},
@@ -59,7 +61,7 @@
             counts_ref.at[pl.ds(cuts[h], cuts[h + 1] - cuts[h]), 0, :],
             staged.at[pl.ds(cuts[h], cuts[h + 1] - cuts[h]), :], load_sem.at[h],
         )
-        for h in range(2)
+        for h in range(parts)
     ]
     for dma in loads:
         dma.start()
@@ -87,13 +89,13 @@
         if mine:
             pl.when((z <= zi) & (zi < last))(lambda: act(copy(UP, z, g, h)))
             pl.when((z >= zi) & (zi > 0))(lambda: act(copy(DOWN, z, g, h)))
-            if h == 0:
+            if h < m:
                 act(copy(ACROSS, z, g, h))
             else:
                 by_line = ((z == 0) & (zi != 0)) | ((z == last) & (zi != last))
                 pl.when(jnp.logical_not(by_line))(lambda: act(copy(ACROSS, z, g, h)))
             pl.when(owner)(lambda: act(rows_copy(z, h)))
-        elif h == 1:
+        elif h >= m:
             pl.when((z == 0) & (zi < last))(lambda: act(copy(UP, z, g, h)))
             pl.when((z == last) & (zi > 0))(lambda: act(copy(DOWN, z, g, h)))
         act(copy(SIB, z, g, h))
@@ -113,7 +115,7 @@
         return z, valid
 
     def forward(d):
-        for h in range(2):
+        for h in range(parts):
             for side in range(2):
                 z, valid = place(d, side)
 
@@ -126,11 +128,12 @@
         for z, hit in ((0, zi == d - 1), (last, last - zi == d - 1)):
             @pl.when(hit)
             def _():
-                arrive(z, g_across, 1)
-                sends(z, False, 1, start)
-
-    def turn(z, h):
-        for k in range(cuts[h], cuts[h + 1], 128):
+                for h in range(m, parts):
+                    arrive(z, g_across, h)
+                    sends(z, False, h, start)
+
+    def turn(z):
+        for k in range(0, cuts[-1], 128):
             @pl.when(owner)
             def _():
                 turned[z, :, k:k + 128] = xs[z, gi, k:k + 128, pl.ds(own_col, rows)].T
@@ -139,18 +142,15 @@
             def _():
                 turned[z, :, k:k + 128] = landed[z, k:k + 128, :].T
 
-    def multiply(z, g, h):
-        tiles = width // TILE
-
+    def multiply(z, a, lo, hi):
         def body(i, carry):
-            a = (g // 2) * 2 + i // tiles
-            n = pl.ds(pl.multiple_of((i % tiles) * TILE, TILE), TILE)
+            n = pl.ds(pl.multiple_of(i * TILE, TILE), TILE)
             acc[a, :, n] += jnp.dot(
-                turned[z, :, part(h)], xs[z, a, part(h), n], preferred_element_type=jnp.float32
+                turned[z, :, lo:hi], xs[z, a, lo:hi, n], preferred_element_type=jnp.float32
             )
             return carry
 
-        lax.fori_loop(0, 2 * tiles, body, 0)
+        lax.fori_loop(0, width // TILE, body, 0)
 
     def near(d):
         def body(side, carry):
@@ -158,39 +158,55 @@
 
             @pl.when(valid)
             def _():
-                for h in range(2):
-                    pl.when(jnp.logical_not(owner))(lambda: rows_copy(z, h).wait_recv())
-                    turn(z, h)
+                @pl.when(jnp.logical_not(owner))
+                def _():
+                    for h in range(parts):
+                        rows_copy(z, h).wait_recv()
+
+                turn(z)
+                multiply(z, gi, 0, cuts[-1])
+                for h in range(parts):
                     arrive(z, g_sib, h)
-                    multiply(z, gi, h)
+                multiply(z, g_sib, 0, cuts[-1])
             return carry
 
         lax.fori_loop(0, 2, body, 0)
+
+    def deliver(a):
+        acc[a] = acc[a] * (1.0 / (nz * cuts[-1]))
+        pltpu.make_async_copy(acc.at[a], out_ref.at[:, a, :], out_sem.at[a]).start()
 
     def far(d):
         def body(side, carry):
             z, valid = place(d, side)
+            at_end = (z == 0) | (z == last)
 
             def take(h):
                 arrive(z, g_across, h)
                 start(copy(SIB, z, g_across, h))
 
-            def use(h):
-                arrive(z, (1 - x) * 2 + (1 - c), h)
-                multiply(z, g_across, h)
-
-            at_end = (z == 0) | (z == last)
-
-            @pl.when(valid)
-            def _():
-                pl.when(at_end)(lambda: use(1))
-                take(0)
-                use(0)
-
-                @pl.when(jnp.logical_not(at_end))
-                def _():
-                    take(1)
-                    use(1)
+            @pl.when(valid & jnp.logical_not(at_end))
+            def _():
+                for h in range(parts):
+                    take(h)
+                multiply(z, g_across, 0, cuts[-1])
+                for h in range(parts):
+                    arrive(z, g_other, h)
+                multiply(z, g_other, 0, cuts[-1])
+
+            @pl.when(valid & at_end)
+            def _():
+                order = sorted(range(parts), key=lambda h: (h - m + 0.5 if h >= m else h))
+                for h in order:
+                    if h < m:
+                        take(h)
+                    else:
+                        pl.when(d == last)(lambda: take(h))
+                    multiply(z, g_across, cuts[h], cuts[h + 1])
+                    if h == order[-1]:
+                        pl.when(d == last)(lambda: deliver(g_across))
+                    arrive(z, g_other, h)
+                    multiply(z, g_other, cuts[h], cuts[h + 1])
             return carry
 
         lax.fori_loop(0, 2, body, 0)
@@ -214,7 +230,7 @@
         return carry
 
     sums[...] = jnp.zeros_like(sums)
-    for h in range(2):
+    for h in range(parts):
         loads[h].wait()
         lax.fori_loop(cuts[h] // 128, cuts[h + 1] // 128, add_up, 0)
     ends_of_line = (zi == 0).astype(jnp.int32) + (zi == last).astype(jnp.int32)
@@ -234,14 +250,10 @@
     for i in range(len(peers)):
         whole += heard[i]
     sums[...] = whole
-    for h in range(2):
+    for h in range(parts):
         lax.fori_loop(cuts[h] // 128, cuts[h + 1] // 128, standardize_rows, 0)
         sends(zi, True, h, start)
     acc[...] = jnp.zeros_like(acc)
-
-    def deliver(a):
-        acc[a] = acc[a] * (1.0 / (nz * cuts[2]))
-        pltpu.make_async_copy(acc.at[a], out_ref.at[:, a, :], out_sem.at[a]).start()
 
     def step(d, carry):
         @pl.when(d == nz)
@@ -250,17 +262,17 @@
             deliver(g_sib)
 
         pl.when((d > 0) & (d < nz))(lambda: forward(d))
-        ends(d)
+        pl.when(d < nz)(lambda: ends(d))
         pl.when(d < nz)(lambda: near(d))
         pl.when(d > 0)(lambda: far(d - 1))
         return carry
 
     lax.fori_loop(0, nz + 1, step, 0)
-    deliver(g_across)
-    deliver((1 - x) * 2 + (1 - c))
+    pl.when((zi > 0) & (zi < last))(lambda: deliver(g_across))
+    deliver(g_other)
 
     def drain(z, carry):
-        for h in range(2):
+        for h in range(parts):
             for mine in (True, False):
                 sends(z, mine, h, finish)
         return carry
@@ -289,10 +301,10 @@
     nz, n_grow = lax.axis_size("cells"), lax.axis_size("grow")
     cell_rows, width = counts.shape[0], counts.shape[3]
     rows = 2 * width // nz
-    cuts = (0, cell_rows // 256 * 128, cell_rows)
+    cuts, m = (0, 256, 512, 640, 896, cell_rows), 3
     flops = 2 * rows * n_grow * width * nz * cell_rows
     scaled = pl.pallas_call(
-        functools.partial(gram_kernel, nz, rows, cuts),
+        functools.partial(gram_kernel, nz, rows, cuts, m),
         out_shape=jax.ShapeDtypeStruct((rows, n_grow, width), jnp.float32),
         in_specs=[
             pl.BlockSpec(memory_space=pl.ANY),
@@ -308,13 +320,13 @@
             pltpu.VMEM((nz, cell_rows, rows), jnp.bfloat16),
             pltpu.VMEM((nz, rows, cell_rows), jnp.bfloat16),
             pltpu.VMEM((n_grow, rows, width), jnp.float32),
-            pltpu.SemaphoreType.DMA((2,)),
+            pltpu.SemaphoreType.DMA((len(cuts) - 1,)),
             pltpu.SemaphoreType.DMA((7,)),
             pltpu.SemaphoreType.DMA((7,)),
-            pltpu.SemaphoreType.DMA((nz, n_grow, 2)),
-            pltpu.SemaphoreType.DMA((4, nz, 2, 2)),
-            pltpu.SemaphoreType.DMA((nz, 2)),
-            pltpu.SemaphoreType.DMA((nz, 2)),
+            pltpu.SemaphoreType.DMA((nz, n_grow, len(cuts) - 1)),
+            pltpu.SemaphoreType.DMA((4, nz, 2, len(cuts) - 1)),
+            pltpu.SemaphoreType.DMA((nz, len(cuts) - 1)),
+            pltpu.SemaphoreType.DMA((nz, len(cuts) - 1)),
             pltpu.SemaphoreType.DMA((n_grow,)),
         ],
         compiler_params=pltpu.CompilerParams(

time: 214 us -> 205 us (0.958)
  Pallas kernels: 214 us -> 204 us
    pallas_call x1, Pallas kernels: 207 us -> 198 us  [line_plan(): pl.pallas_call(functools.partial(gram_kernel, nz, rows, cuts, m), out_sha...]
where the time goes in v4:
time: 205 us; the launch traced here: 204 us
  Pallas kernels  204 us (100%)
    pallas_call x1, Pallas kernels, line_plan(): pl.pallas_call(functools.partial(gram_kernel, nz, rows, cuts, m), out_sha...  198 us
    pallas_call x1, Pallas kernels, line_plan(): pl.pallas_call(copy_kernel, out_shape=jax.ShapeDtypeStruct(scaled.shape,...  6.57 us

profile of v4, /device:TPU:4, one launch (start us, length us, event | category | flops | bytes accessed | tf_op | source)
XLA Modules:
  0.0 204.3 jit_solution(15813653908060532588)
XLA Ops:
  0.0 197.8 %shard_map.37.src = f32[512,4,1024]{2,1,0:T(4,128)} custom-call(s32[1152,1,1024]{2,1,0:T(1,128)} %bitcast.6, f32[1,1024]{1,0:T(1,128)} %bitcast.7, f32[1,1024]{1,0:T(1,128)} %bitcast.8), custom_call_target="tpu_custom_call" | custom-call | flops 19327352832 | bytes 8388608 | tf_op jit(solution)/shard_map/pallas_call | solution.py:306
  197.8 6.6 %shard_map.38 = f32[512,4,1024]{2,1,0:T(4,128)} custom-call(f32[512,4,1024]{2,1,0:T(4,128)} %shard_map.37.src), custom_call_target="tpu_custom_call" | custom-call | tf_op jit(solution)/shard_map/pallas_call | solution.py:339

commit v5 on v4

--- a/solution.py
+++ b/solution.py
@@ -11,6 +11,7 @@
 MESH = pl.DeviceIdType.MESH
 SIB, UP, DOWN, ACROSS = range(4)
 TILE = 256
+LEVELS = 32767.0
 
 
 def standardize(counts, gene_mean, gene_scale):
@@ -24,8 +25,9 @@
 
 
 def gram_kernel(nz, rows, cuts, m, counts_ref, mean_ref, scale_ref, out_ref,
-                staged, sums, heard, xs, landed, turned, acc,
-                load_sem, sums_recv, sums_send, recv_sem, send_sem, rows_recv, rows_send, out_sem):
+                staged, sums, heard, xs, landed, turned, acc, told, asked, told_unit, asked_unit,
+                load_sem, sums_recv, sums_send, recv_sem, send_sem, rows_recv, rows_send, out_sem,
+                more_recv, more_send, asked_sem, told_sem):
     zi, gi, yi = lax.axis_index("cells"), lax.axis_index("grow"), lax.axis_index("gcol")
     width = xs.shape[3]
     last = nz - 1
@@ -42,6 +44,9 @@
     }
     owner = (zi * 2) // nz == yi
     own_col = pl.multiple_of((zi % (nz // 2)) * rows, rows)
+    rest_col = pl.multiple_of(rows - (zi % (nz // 2)) * rows, rows)
+    tip = (zi == 0) | (zi == last)
+    far_end = jnp.where(zi == 0, last, 0)
 
     barrier = pltpu.get_barrier_semaphore()
 
@@ -69,13 +74,31 @@
     def part(h):
         return pl.ds(cuts[h], cuts[h + 1] - cuts[h])
 
-    def copy(kind, z, g, h):
-        ref = xs.at[z, g, part(h), :]
+    def copy(kind, z, g, h, narrow=False):
+        ref = xs.at[z, g, part(h), pl.ds(own_col, rows)] if narrow else xs.at[z, g, part(h), :]
         return pltpu.make_async_remote_copy(
             src_ref=ref, dst_ref=ref,
             send_sem=send_sem.at[kind, z, g // 2, h], recv_sem=recv_sem.at[z, g, h],
             device_id=target[kind], device_id_type=MESH,
         )
+
+    def more_copy(z, h, i):
+        return pltpu.make_async_remote_copy(
+            src_ref=xs.at[z, g_across, part(h), pl.ds(own_col, rows)],
+            dst_ref=xs.at[z, g_across, part(h), pl.ds(rest_col, rows)],
+            send_sem=more_send.at[i, h], recv_sem=more_recv.at[i, h],
+            device_id={"gcol": 1 - yi}, device_id_type=MESH,
+        )
+
+    def answer(i):
+        return [
+            pltpu.make_async_remote_copy(
+                src_ref=src.at[i], dst_ref=dst.at[i],
+                send_sem=told_sem.at[i, j], recv_sem=asked_sem.at[i, j],
+                device_id=target[ACROSS], device_id_type=MESH,
+            )
+            for j, (src, dst) in enumerate(((told_unit, asked_unit), (told, asked)))
+        ]
 
     def rows_copy(z, h):
         return pltpu.make_async_remote_copy(
@@ -89,16 +112,27 @@
         if mine:
             pl.when((z <= zi) & (zi < last))(lambda: act(copy(UP, z, g, h)))
             pl.when((z >= zi) & (zi > 0))(lambda: act(copy(DOWN, z, g, h)))
-            if h < m:
-                act(copy(ACROSS, z, g, h))
-            else:
-                by_line = ((z == 0) & (zi != 0)) | ((z == last) & (zi != last))
-                pl.when(jnp.logical_not(by_line))(lambda: act(copy(ACROSS, z, g, h)))
+            by_line = ((z == 0) & (zi != 0)) | ((z == last) & (zi != last))
+            some = tip & (z - zi <= 1) & (zi - z <= 1)
+            if h >= m:
+                some = some & (z != zi)
+            pl.when(some)(lambda: act(copy(ACROSS, z, g, h, True)))
+            whole = jnp.logical_not(some)
+            if h >= m:
+                whole = whole & jnp.logical_not(by_line)
+            pl.when(whole)(lambda: act(copy(ACROSS, z, g, h)))
             pl.when(owner)(lambda: act(rows_copy(z, h)))
         elif h >= m:
             pl.when((z == 0) & (zi < last))(lambda: act(copy(UP, z, g, h)))
             pl.when((z == last) & (zi > 0))(lambda: act(copy(DOWN, z, g, h)))
-        act(copy(SIB, z, g, h))
+        if mine:
+            act(copy(SIB, z, g, h))
+        else:
+            some = tip & (z - zi <= 1) & (zi - z <= 1)
+            if h >= m:
+                some = some & (z != zi)
+            pl.when(some)(lambda: act(copy(SIB, z, g, h, True)))
+            pl.when(jnp.logical_not(some))(lambda: act(copy(SIB, z, g, h)))
 
     def start(dma):
         dma.start()
@@ -106,8 +140,8 @@
     def finish(dma):
         dma.wait_send()
 
-    def arrive(z, g, h):
-        copy(SIB, z, g, h).wait_recv()
+    def arrive(z, g, h, narrow=False):
+        copy(SIB, z, g, h, narrow).wait_recv()
 
     def place(d, side):
         z = zi - d + 2 * d * side
@@ -132,25 +166,34 @@
                     arrive(z, g_across, h)
                     sends(z, False, h, start)
 
-    def turn(z):
-        for k in range(0, cuts[-1], 128):
+    def turn(z, g, into, first, end, there):
+        def body(k, carry):
+            r = pl.ds(pl.multiple_of(k * 128, 128), 128)
+
             @pl.when(owner)
             def _():
-                turned[z, :, k:k + 128] = xs[z, gi, k:k + 128, pl.ds(own_col, rows)].T
+                turned[into, :, r] = xs[z, g, r, pl.ds(own_col, rows)].T
 
             @pl.when(jnp.logical_not(owner))
             def _():
-                turned[z, :, k:k + 128] = landed[z, k:k + 128, :].T
-
-    def multiply(z, a, lo, hi):
+                turned[into, :, r] = there(r).T
+            return carry
+
+        lax.fori_loop(first // 128, end // 128, body, 0)
+
+    def multiply(z, g, lo, hi, both=False, col=0, wide=None, theirs=False):
+        tiles = (wide or width) // TILE
+
         def body(i, carry):
-            n = pl.ds(pl.multiple_of(i * TILE, TILE), TILE)
-            acc[a, :, n] += jnp.dot(
-                turned[z, :, lo:hi], xs[z, a, lo:hi, n], preferred_element_type=jnp.float32
+            a = (g // 2) * 2 + (g + i // tiles) % 2
+            n = pl.ds(pl.multiple_of(col + (i % tiles) * TILE, TILE), TILE)
+            into, left = (a + 2) % 4 if theirs else a, far_end if theirs else z
+            acc[into, :, n] += jnp.dot(
+                turned[left, :, lo:hi], xs[z, a, lo:hi, n], preferred_element_type=jnp.float32
             )
             return carry
 
-        lax.fori_loop(0, width // TILE, body, 0)
+        lax.fori_loop(0, tiles * (2 if both else 1), body, 0)
 
     def near(d):
         def body(side, carry):
@@ -163,18 +206,76 @@
                     for h in range(parts):
                         rows_copy(z, h).wait_recv()
 
-                turn(z)
-                multiply(z, gi, 0, cuts[-1])
+                turn(z, gi, z, 0, cuts[-1], lambda r: landed[z, r, :])
                 for h in range(parts):
                     arrive(z, g_sib, h)
-                multiply(z, g_sib, 0, cuts[-1])
+                multiply(z, gi, 0, cuts[-1], both=True)
             return carry
 
         lax.fori_loop(0, 2, body, 0)
 
     def deliver(a):
-        acc[a] = acc[a] * (1.0 / (nz * cuts[-1]))
+        def scale(k, carry):
+            r = pl.ds(pl.multiple_of(k * 64, 64), 64)
+            acc[a, r, :] = acc[a, r, :] * (1.0 / (nz * cuts[-1]))
+            return carry
+
+        lax.fori_loop(0, rows // 64, scale, 0)
         pltpu.make_async_copy(acc.at[a], out_ref.at[:, a, :], out_sem.at[a]).start()
+
+    def tip_far(z, d):
+        def each(h, act):
+            act(h) if h < m else pl.when(d == 1)(lambda: act(h))
+
+        def take(h):
+            arrive(z, g_across, h, True)
+            start(copy(SIB, z, g_across, h, True))
+            pl.when(owner)(lambda: more_copy(z, h, d).start())
+
+        for h in range(parts):
+            each(h, take)
+        def wait_more(h):
+            pl.when(jnp.logical_not(owner))(lambda: more_copy(z, h, d).wait_recv())
+
+        for h in range(parts):
+            each(h, wait_more)
+
+        def theirs(lo, hi):
+            turn(z, g_across, far_end, lo, hi, lambda r: xs[z, g_across, r, pl.ds(rest_col, rows)])
+            multiply(z, gi, lo, hi, True, rest_col, rows, True)
+
+        theirs(0, cuts[m])
+
+        @pl.when(d == 1)
+        def _():
+            theirs(cuts[m], cuts[-1])
+            for i, a in enumerate((g_across, g_other)):
+                def code(j, carry):
+                    col = pl.ds(pl.multiple_of(rest_col + j * 128, 128), 128)
+                    at = pl.ds(pl.multiple_of(j * 128, 128), 128)
+                    sent = acc[a, :, col]
+                    top = jnp.maximum(jnp.max(jnp.abs(sent), axis=0, keepdims=True), 1e-30)
+                    whole = jnp.floor(sent * (LEVELS / top) + 0.5).astype(jnp.int32)
+                    told[i, :, at] = whole.astype(jnp.int16)
+                    told_unit[i, :, at] = jnp.broadcast_to(top * (1.0 / LEVELS), (8, 128))
+                    acc[a, :, col] = jnp.zeros((rows, 128), jnp.float32)
+                    return carry
+
+                lax.fori_loop(0, rows // 128, code, 0)
+                for dma in answer(i):
+                    dma.start()
+
+        for h in range(parts):
+            if h < m:
+                arrive(z, g_other, h, True)
+            else:
+                pl.when(d == 1)(lambda: arrive(z, g_other, h, True))
+                pl.when(d == 0)(lambda: arrive(z, g_other, h))
+        multiply(z, g_across, 0, cuts[-1], True, own_col, rows)
+
+        @pl.when(d == 1)
+        def _():
+            multiply(zi, g_across, cuts[m], cuts[-1], True, rest_col, rows)
 
     def far(d):
         def body(side, carry):
@@ -185,16 +286,19 @@
                 arrive(z, g_across, h)
                 start(copy(SIB, z, g_across, h))
 
-            @pl.when(valid & jnp.logical_not(at_end))
+            @pl.when(valid & tip & (d <= 1))
+            def _():
+                tip_far(z, d)
+
+            @pl.when(valid & jnp.logical_not(at_end) & jnp.logical_not(tip & (d <= 1)))
             def _():
                 for h in range(parts):
                     take(h)
-                multiply(z, g_across, 0, cuts[-1])
                 for h in range(parts):
                     arrive(z, g_other, h)
-                multiply(z, g_other, 0, cuts[-1])
-
-            @pl.when(valid & at_end)
+                multiply(z, g_across, 0, cuts[-1], both=True)
+
+            @pl.when(valid & at_end & jnp.logical_not(tip & (d <= 1)))
             def _():
                 order = sorted(range(parts), key=lambda h: (h - m + 0.5 if h >= m else h))
                 for h in order:
@@ -202,11 +306,14 @@
                         take(h)
                     else:
                         pl.when(d == last)(lambda: take(h))
-                    multiply(z, g_across, cuts[h], cuts[h + 1])
-                    if h == order[-1]:
+                    if h != order[-1]:
+                        arrive(z, g_other, h)
+                        multiply(z, g_across, cuts[h], cuts[h + 1], both=True)
+                    else:
+                        multiply(z, g_across, cuts[h], cuts[h + 1])
                         pl.when(d == last)(lambda: deliver(g_across))
-                    arrive(z, g_other, h)
-                    multiply(z, g_other, cuts[h], cuts[h + 1])
+                        arrive(z, g_other, h)
+                        multiply(z, g_other, cuts[h], cuts[h + 1])
             return carry
 
         lax.fori_loop(0, 2, body, 0)
@@ -253,7 +360,13 @@
     for h in range(parts):
         lax.fori_loop(cuts[h] // 128, cuts[h + 1] // 128, standardize_rows, 0)
         sends(zi, True, h, start)
-    acc[...] = jnp.zeros_like(acc)
+
+    def clear(k, carry):
+        acc[k // 8, pl.ds((k % 8) * (rows // 8), rows // 8), :] = jnp.zeros(
+            (rows // 8, width), jnp.float32)
+        return carry
+
+    lax.fori_loop(0, acc.shape[0] * 8, clear, 0)
 
     def step(d, carry):
         @pl.when(d == nz)
@@ -261,6 +374,20 @@
             deliver(gi)
             deliver(g_sib)
 
+            @pl.when(tip)
+            def _():
+                for i, a in enumerate((g_across, g_other)):
+                    for dma in answer(i):
+                        dma.wait()
+                    def decode(j, carry):
+                        col = pl.ds(pl.multiple_of(rest_col + j * 128, 128), 128)
+                        at = pl.ds(pl.multiple_of(j * 128, 128), 128)
+                        got = asked[i, :, at].astype(jnp.int32).astype(jnp.float32)
+                        acc[a, :, col] += got * asked_unit[i, 0:1, at]
+                        return carry
+
+                    lax.fori_loop(0, rows // 128, decode, 0)
+
         pl.when((d > 0) & (d < nz))(lambda: forward(d))
         pl.when(d < nz)(lambda: ends(d))
         pl.when(d < nz)(lambda: near(d))
@@ -278,6 +405,14 @@
         return carry
 
     lax.fori_loop(0, nz, drain, 0)
+
+    @pl.when(tip & owner)
+    def _():
+        for h in range(parts):
+            if h < m:
+                more_copy(zi, h, 0).wait_send()
+            more_copy(jnp.where(zi == 0, 1, last - 1), h, 1).wait_send()
+
     for a in range(acc.shape[0]):
         pltpu.make_async_copy(acc.at[a], out_ref.at[:, a, :], out_sem.at[a]).wait()
 
@@ -301,7 +436,7 @@
     nz, n_grow = lax.axis_size("cells"), lax.axis_size("grow")
     cell_rows, width = counts.shape[0], counts.shape[3]
     rows = 2 * width // nz
-    cuts, m = (0, 256, 512, 640, 896, cell_rows), 3
+    cuts, m = (0, 384, 640, 768, 1024, cell_rows), 3
     flops = 2 * rows * n_grow * width * nz * cell_rows
     scaled = pl.pallas_call(
         functools.partial(gram_kernel, nz, rows, cuts, m),
@@ -320,6 +455,10 @@
             pltpu.VMEM((nz, cell_rows, rows), jnp.bfloat16),
             pltpu.VMEM((nz, rows, cell_rows), jnp.bfloat16),
             pltpu.VMEM((n_grow, rows, width), jnp.float32),
+            pltpu.VMEM((2, rows, rows), jnp.int16),
+            pltpu.VMEM((2, rows, rows), jnp.int16),
+            pltpu.VMEM((2, 8, rows), jnp.float32),
+            pltpu.VMEM((2, 8, rows), jnp.float32),
             pltpu.SemaphoreType.DMA((len(cuts) - 1,)),
             pltpu.SemaphoreType.DMA((7,)),
             pltpu.SemaphoreType.DMA((7,)),
@@ -328,9 +467,13 @@
             pltpu.SemaphoreType.DMA((nz, len(cuts) - 1)),
             pltpu.SemaphoreType.DMA((nz, len(cuts) - 1)),
             pltpu.SemaphoreType.DMA((n_grow,)),
+            pltpu.SemaphoreType.DMA((2, len(cuts) - 1)),
+            pltpu.SemaphoreType.DMA((2, len(cuts) - 1)),
+            pltpu.SemaphoreType.DMA((2, 2)),
+            pltpu.SemaphoreType.DMA((2, 2)),
         ],
         compiler_params=pltpu.CompilerParams(
-            collective_id=0, has_side_effects=True, vmem_limit_bytes=62 * 2**20
+            collective_id=0, has_side_effects=True, vmem_limit_bytes=63 * 2**20
         ),
         cost_estimate=pl.CostEstimate(
             flops=flops, bytes_accessed=4 * rows * n_grow * width, transcendentals=0

time: 205 us -> 224 us (1.093)
  Pallas kernels: 204 us -> 223 us
    pallas_call x1, Pallas kernels: 198 us -> 216 us  [line_plan(): pl.pallas_call(functools.partial(gram_kernel, nz, rows, cuts, m), out_sha...]
where the time goes in v5:
time: 224 us; the launch traced here: 223 us
  Pallas kernels  223 us (100%)
    pallas_call x1, Pallas kernels, line_plan(): pl.pallas_call(functools.partial(gram_kernel, nz, rows, cuts, m), out_sha...  216 us
    pallas_call x1, Pallas kernels, line_plan(): pl.pallas_call(copy_kernel, out_shape=jax.ShapeDtypeStruct(scaled.shape,...  6.57 us

profile of v5, /device:TPU:4, one launch (start us, length us, event | category | flops | bytes accessed | tf_op | source)
XLA Modules:
  0.0 222.9 jit_solution(14411215421017283196)
XLA Ops:
  0.0 216.3 %shard_map.37.src = f32[512,4,1024]{2,1,0:T(4,128)} custom-call(s32[1152,1,1024]{2,1,0:T(1,128)} %bitcast.6, f32[1,1024]{1,0:T(1,128)} %bitcast.7, f32[1,1024]{1,0:T(1,128)} %bitcast.8), custom_call_target="tpu_custom_call" | custom-call | flops 19327352832 | bytes 8388608 | tf_op jit(solution)/shard_map/pallas_call | solution.py:441
  216.3 6.6 %shard_map.38 = f32[512,4,1024]{2,1,0:T(4,128)} custom-call(f32[512,4,1024]{2,1,0:T(4,128)} %shard_map.37.src), custom_call_target="tpu_custom_call" | custom-call | tf_op jit(solution)/shard_map/pallas_call | solution.py:482

commit v6 on v5

--- a/solution.py
+++ b/solution.py
@@ -223,9 +223,11 @@
         lax.fori_loop(0, rows // 64, scale, 0)
         pltpu.make_async_copy(acc.at[a], out_ref.at[:, a, :], out_sem.at[a]).start()
 
-    def tip_far(z, d):
-        def each(h, act):
-            act(h) if h < m else pl.when(d == 1)(lambda: act(h))
+    def each(h, d, act):
+        act(h) if h < m else pl.when(d == 1)(lambda: act(h))
+
+    def tip_take(d):
+        z = jnp.where(zi == 0, d, last - d)
 
         def take(h):
             arrive(z, g_across, h, True)
@@ -233,12 +235,14 @@
             pl.when(owner)(lambda: more_copy(z, h, d).start())
 
         for h in range(parts):
-            each(h, take)
+            each(h, d, take)
+
+    def tip_far(z, d):
         def wait_more(h):
             pl.when(jnp.logical_not(owner))(lambda: more_copy(z, h, d).wait_recv())
 
         for h in range(parts):
-            each(h, wait_more)
+            each(h, d, wait_more)
 
         def theirs(lo, hi):
             turn(z, g_across, far_end, lo, hi, lambda r: xs[z, g_across, r, pl.ds(rest_col, rows)])
@@ -390,8 +394,9 @@
 
         pl.when((d > 0) & (d < nz))(lambda: forward(d))
         pl.when(d < nz)(lambda: ends(d))
+        pl.when(d > 0)(lambda: far(d - 1))
         pl.when(d < nz)(lambda: near(d))
-        pl.when(d > 0)(lambda: far(d - 1))
+        pl.when(tip & (d < 2))(lambda: tip_take(d))
         return carry
 
     lax.fori_loop(0, nz + 1, step, 0)

time: 224 us -> 208 us (0.929)
  Pallas kernels: 223 us -> 207 us
    pallas_call x1, Pallas kernels: 216 us -> 201 us  [line_plan(): pl.pallas_call(functools.partial(gram_kernel, nz, rows, cuts, m), out_sha...]
where the time goes in v6:
time: 208 us; the launch traced here: 207 us
  Pallas kernels  207 us (100%)
    pallas_call x1, Pallas kernels, line_plan(): pl.pallas_call(functools.partial(gram_kernel, nz, rows, cuts, m), out_sha...  201 us
    pallas_call x1, Pallas kernels, line_plan(): pl.pallas_call(copy_kernel, out_shape=jax.ShapeDtypeStruct(scaled.shape,...  6.57 us

profile of v6, /device:TPU:4, one launch (start us, length us, event | category | flops | bytes accessed | tf_op | source)
XLA Modules:
  0.0 207.3 jit_solution(7962857908406114901)
XLA Ops:
  0.0 200.7 %shard_map.37.src = f32[512,4,1024]{2,1,0:T(4,128)} custom-call(s32[1152,1,1024]{2,1,0:T(1,128)} %bitcast.6, f32[1,1024]{1,0:T(1,128)} %bitcast.7, f32[1,1024]{1,0:T(1,128)} %bitcast.8), custom_call_target="tpu_custom_call" | custom-call | flops 19327352832 | bytes 8388608 | tf_op jit(solution)/shard_map/pallas_call | solution.py:446
  200.7 6.6 %shard_map.38 = f32[512,4,1024]{2,1,0:T(4,128)} custom-call(f32[512,4,1024]{2,1,0:T(4,128)} %shard_map.37.src), custom_call_target="tpu_custom_call" | custom-call | tf_op jit(solution)/shard_map/pallas_call | solution.py:487
